TPU v7x, 1024 devices: a whole 8x8x8 slice. The times are simulated.
1024 devices in a mesh: owner: 64 (over x, z), dp: 16 (over y, core).
Axes of the slice: x: 8, y: 8, z: 8, core: 2. Of those that a mesh axis runs over, the one named last changes fastest.
Arguments:
- grads: bfloat16 [16, 48, 16, 64, 1024], P('dp', None, None, 'owner'), may hold values from -6 to 6
- owner_map: int32 [48], replicated, may hold values from 0 to 63, as said below
- block_dims: int32 [48, 2], replicated, may hold values from 1 to 8
- left_root: bfloat16 [64, 2, 1024, 1024], P('owner'), may hold values from -0.3 to 2, as said below
- right_root: bfloat16 [64, 2, 1024, 1024], P('owner'), may hold values from -0.3 to 2, as said below
Outputs:
- direction: bfloat16 [48, 16, 64, 1024], P(None, 'dp', 'owner')
Inputs may be any that keep to these rules, and one draw needn't show every extreme that they name: `owner_map`: every owner column owns 0, 1 or 2 blocks, and some column owns exactly 2. `left_root`: each matrix is symmetric. `right_root`: each matrix is symmetric.
All inputs are finite; a program needn't handle non-finite values.
Results may differ from a plain program's by a relative error of at most 0.0057.
Values may be sent and summed in bfloat16 or wider, within the bound.
A program may use at most 32 MiB of HBM per device.

v0:
```python
import jax
import jax.numpy as jnp
from jax import lax
from jax.sharding import PartitionSpec as P


def owner_slots(owner_map):
    block_count = owner_map.shape[0]
    same_owner = owner_map[:, None] == owner_map[None, :]
    earlier = jnp.arange(block_count)[None, :] < jnp.arange(block_count)[:, None]
    return jnp.sum((same_owner & earlier).astype(jnp.int32), axis=1)


def on_device(grads, owner_map, block_dims, left_root, right_root):
    owners = lax.axis_size("owner")
    groups = lax.axis_size("dp")
    block_count = owner_map.shape[0]
    block_order = left_root.shape[2]
    slot_count = left_root.shape[1]
    piece_len = grads.shape[4]
    slab_rows = block_order // groups
    tile_len = block_order // 8
    replica_terms = grads[0].astype(jnp.float32)
    summed = lax.psum_scatter(replica_terms, "dp", scatter_dimension=1, tiled=True)
    pieces = summed.reshape(block_count, piece_len).astype(jnp.bfloat16)
    slot_of = owner_slots(owner_map)
    target = slot_of * owners + owner_map
    chooser = (jnp.arange(slot_count * owners)[:, None] == target[None, :]).astype(jnp.bfloat16)
    outgoing = jnp.dot(chooser, pieces, preferred_element_type=jnp.float32)
    outgoing = outgoing.astype(jnp.bfloat16).reshape(slot_count, owners, piece_len)
    incoming = lax.all_to_all(outgoing, "owner", split_axis=1, concat_axis=1, tiled=True)
    my_owner = lax.axis_index("owner")
    dp_index = lax.axis_index("dp")
    owned_slot = (owner_map[None, :] == my_owner) & (
        slot_of[None, :] == jnp.arange(slot_count)[:, None]
    )
    live_rows = jnp.sum(jnp.where(owned_slot, block_dims[:, 0][None, :], 0), axis=1) * tile_len
    live_cols = jnp.sum(jnp.where(owned_slot, block_dims[:, 1][None, :], 0), axis=1) * tile_len
    row_ids = dp_index * slab_rows + jnp.arange(slab_rows)
    col_ids = jnp.arange(block_order)
    live_mask = (row_ids[None, :, None] < live_rows[:, None, None]) & (
        col_ids[None, None, :] < live_cols[:, None, None]
    )
    masked = jnp.where(live_mask, incoming, jnp.zeros((), incoming.dtype))
    left_full = left_root[0]
    right_full = right_root[0]
    left_rows = lax.dynamic_slice_in_dim(left_full, dp_index * slab_rows, slab_rows, 1)
    product = jnp.einsum(
        "csk,ckn->csn",
        left_rows,
        lax.all_gather(masked, "dp", axis=1, tiled=True),
        preferred_element_type=jnp.float32,
    )
    product_rows = product.astype(jnp.bfloat16)
    update = jnp.einsum(
        "csk,ckn->csn", product_rows, right_full, preferred_element_type=jnp.float32
    )
    update = jnp.where(live_mask, update, jnp.zeros((), jnp.float32)).astype(jnp.bfloat16)
    returned = lax.all_to_all(update, "owner", split_axis=1, concat_axis=1, tiled=True)
    direction_rows = jnp.dot(
        chooser.T,
        returned.reshape(slot_count * owners, piece_len),
        preferred_element_type=jnp.float32,
    )
    return direction_rows.astype(jnp.bfloat16).reshape(block_count, 1, 1, piece_len)


def solution(mesh):
    placed = (
        P("dp", None, None, "owner", None),
        P(),
        P(),
        P("owner", None, None, None),
        P("owner", None, None, None),
    )
    return jax.shard_map(
        on_device,
        mesh=mesh,
        in_specs=placed,
        out_specs=P(None, "dp", "owner", None),
        check_vma=False,
    )
```

profile of v0, /device:TPU:1, one launch (start us, length us, event | category | flops | bytes accessed | tf_op | source)
XLA Modules:
  0.0 197.6 jit_solution(13066144051245086934)
XLA Ops:
  6.5 0.0 copy-start.1
  6.5 0.0 copy-start
  6.5 0.0 reduce-scatter.2.cloned.1.call-start
  6.5 4.0 %bitcast_convert_fusion = f32[48,16,1,1024]{3,0,2,1:T(8,128)} fusion(bf16[1,48,16,1,1024]{4,2,3,1,0:T(8,128)(2,1)} %param.5), kind=kLoop, calls=%fused_computation.2 | loop fusion | flops 786432 | bytes 4718592 | tf_op jit(solution)/shard_map/convert_element_type | solution.py:23
  10.5 0.0 reduce-scatter.2.cloned.1.call-update
  10.6 0.0 copy-done.1
  10.6 0.2 convert_reduce_fusion
  10.8 0.0 copy-done
  10.8 0.1 select_reduce_fusion.1
  11.0 77.5 %reduce-scatter.2.cloned.1.call-done = f32[48,1,1,1024]{3,0,2,1:T(8,128)} async-done(((f32[48,16,1,1024]{3,0,2,1:T(8,128)}), f32[48,1,1,1024]{3,0,2,1:T(8,128)}) %reduce-scatter.2.cloned.1.call-update) | async-done | bytes 196624 | tf_op jit(solution)/shard_map/reduce_scatter | solution.py:24
  88.5 1.1 convolution_convert_fusion
  89.6 1.0 copy.17
  90.6 11.1 %all-to-all-start = ((bf16[2,64,1024]{2,0,1:T(2,128)(2,1)}), bf16[2,64,1024]{2,0,1:T(2,128)(2,1)S(1)}, u32[]{:S(2)}, u32[]{:S(2)}) async-start(bf16[2,64,1024]{2,0,1:T(2,128)(2,1)} %copy.17), calls=%async_computation.1 | async-start | bytes 524288 | tf_op jit(solution)/shard_map/all_to_all | solution.py:31
  101.7 0.0 all-gather.2.cloned.1.call-start
  101.7 0.1 broadcast_compare_fusion
  101.8 0.1 iota_compare_fusion.4
  101.9 12.3 %all-to-all-done = bf16[2,64,1024]{2,0,1:T(2,128)(2,1)S(1)} async-done(((bf16[2,64,1024]{2,0,1:T(2,128)(2,1)}), bf16[2,64,1024]{2,0,1:T(2,128)(2,1)S(1)}, u32[]{:S(2)}, u32[]{:S(2)}) %all-to-all-start) | async-done | bytes 262176 | tf_op jit(solution)/shard_map/all_to_all | solution.py:31
  114.2 0.8 and_select_fusion
  115.1 0.0 all-gather.2.cloned.1.call-update
  115.1 42.7 %all-gather.2.cloned.1.call-done = bf16[2,1024,1024]{2,1,0:T(8,128)(2,1)} async-done(((bf16[2,64,1024]{2,1,0:T(8,128)(2,1)}), bf16[2,1024,1024]{2,1,0:T(8,128)(2,1)}) %all-gather.2.cloned.1.call-update) | async-done | bytes 4194320 | tf_op jit(solution)/shard_map/all_gather | solution.py:51
  157.8 5.1 %fusion.5 = bf16[2,64,1024]{2,1,0:T(8,128)(2,1)S(1)} fusion(bf16[1,2,1024,1024]{3,2,1,0:T(8,128)(2,1)} %param.9, bf16[2,1024,1024]{2,1,0:T(8,128)(2,1)} %all-gather.2.cloned.1.call-done, bf16[1,2,1024,1024]{3,2,1,0:T(8,128)(2,1)} %param.8, s32[]{:T(128)S(6)} %select_n.20, pred[2,1024]{1,0:T(4,128)(4,1)S(1)} %iota_compare_fusion.4, ...), kind=kOutput, calls=%fused_computation.6 | convolution fusion | flops 537395200 | bytes 8915076 | tf_op jit(solution)/shard_map/csk,ckn->csn/dot_general | solution.py:55
  162.9 0.3 copy.19
  163.2 26.7 %all_to_all.10 = bf16[2,64,1024]{2,0,1:T(2,128)(2,1)S(1)} all-to-all(bf16[2,64,1024]{2,0,1:T(2,128)(2,1)S(1)} %copy.19), channel_id=1, replica_groups=mesh['owner'=64,'dp'=16] {'owner'}, dimensions={1} | all-to-all | bytes 524288 | tf_op jit(solution)/shard_map/all_to_all | solution.py:59
  189.9 0.9 fusion.8
  (6 shorter events, 0.1 us)
Async XLA Ops:
  6.5 4.0 %copy-start.1 = (s32[48]{0:T(128)S(1)}, s32[48]{0:T(128)}, u32[]{:S(2)}) copy-start(s32[48]{0:T(128)} %param.6) | copy-start | bytes 580
  6.5 4.2 %copy-start = (s32[48,2]{0,1:T(2,128)S(1)}, s32[48,2]{0,1:T(2,128)}, u32[]{:S(2)}) copy-start(s32[48,2]{0,1:T(2,128)} %param.7) | copy-start | bytes 1156
  6.5 82.0 %reduce-scatter.2.cloned.1.call-start = ((), (), s32[]{:S(2)}) async-start(), calls=%async_computation.3 | async-start | bytes 3342336 | tf_op jit(solution)/shard_map/reduce_scatter | solution.py:24
  90.6 23.6 %all-to-all-start = ((bf16[2,64,1024]{2,0,1:T(2,128)(2,1)}), bf16[2,64,1024]{2,0,1:T(2,128)(2,1)S(1)}, u32[]{:S(2)}, u32[]{:S(2)}) async-start(bf16[2,64,1024]{2,0,1:T(2,128)(2,1)} %copy.17), calls=%async_computation.1 | async-start | bytes 524288 | tf_op jit(solution)/shard_map/all_to_all | solution.py:31
  101.7 56.1 %all-gather.2.cloned.1.call-start = ((), (), s32[]{:S(2)}) async-start(), calls=%async_computation.4 | async-start | bytes 4456448 | tf_op jit(solution)/shard_map/all_gather | solution.py:51
Sparse Core Ops, SparseCore 0:
  10.8 77.6 reduce-scatter.1
  115.2 42.5 all-gather.1
where the time goes:
time: 199 us; the launch traced here: 198 us
  waiting for transfers between devices  133 us (67%)
  blocking collectives  26.7 us (13%)
  between operations  13.5 us (7%)
  starting transfers between devices  11.1 us (6%)
  matrix products  7.12 us (4%)
  other arithmetic  5.34 us (3%)
    reduce_scatter x1, waiting for transfers between devices, on_device(): lax.psum_scatter(replica_terms, 'dp', scatter_dimension=1, tiled=True)  77.5 us
    all_gather x1, waiting for transfers between devices, on_device(): lax.all_gather(masked, 'dp', axis=1, tiled=True)  42.7 us
    all_to_all x1, blocking collectives, on_device(): lax.all_to_all(update, 'owner', split_axis=1, concat_axis=1, tiled=True)  26.7 us
    all_to_all x1, waiting for transfers between devices, on_device(): lax.all_to_all(outgoing, 'owner', split_axis=1, concat_axis=1, tiled=True)  12.3 us
    all_to_all x1, starting transfers between devices, on_device(): lax.all_to_all(outgoing, 'owner', split_axis=1, concat_axis=1, tiled=True)  11.1 us
    dot_general x1, matrix products, on_device(): jnp.einsum('csk,ckn->csn', product_rows, right_full, preferred_element_ty...  5.12 us
    convert_element_type x1, other arithmetic, on_device(): replica_terms = grads[0].astype(jnp.float32)  4 us
  transfers between devices with their start and end apart: 3, of which 3 were waited for; matrix products, arithmetic and copies ran while one was open for 0% of the time, Pallas kernels for 0%

commit v1 on v0

v1 whole, which is shorter than its diff:
```python
import functools

import jax
import jax.numpy as jnp
from jax import lax
from jax.experimental import pallas as pl
from jax.experimental.pallas import tpu as pltpu
from jax.sharding import PartitionSpec as P

MESH = pl.DeviceIdType.MESH
F32, BF16, I32 = jnp.float32, jnp.bfloat16, jnp.int32
NB = 48
HALF = NB // 2
NO = 64
NY = 8
LANES = 128
FAR_FIRST = (4, 3, 5, 2, 6, 1, 7)


def remote(src, dst, send_sem, recv_sem, owner, dp):
    return pltpu.make_async_remote_copy(
        src_ref=src, dst_ref=dst, send_sem=send_sem, recv_sem=recv_sem,
        device_id={"owner": owner, "dp": dp}, device_id_type=MESH,
    )


def signal(sem, owner, dp):
    pl.semaphore_signal(sem, inc=1, device_id={"owner": owner, "dp": dp}, device_id_type=MESH)


def diagonal_column(row):
    sub = lax.broadcasted_iota(I32, (LANES, LANES), 0)
    lane = lax.broadcasted_iota(I32, (LANES, LANES), 1)
    return jnp.sum(jnp.where(sub == lane, row, 0), axis=1, keepdims=True)


def build_tables(map_ref, dims_ref, rows, table):
    rows[...] = jnp.full((8, LANES), -1, I32)
    rows[0:1, 0:NB] = map_ref[...]
    rows[1:3, 0:NB] = dims_ref[...]
    sub = lax.broadcasted_iota(I32, (LANES, LANES), 0)
    lane = lax.broadcasted_iota(I32, (LANES, LANES), 1)
    owner_row = rows[0:1, :]
    owner_col = diagonal_column(owner_row)
    live_rows = diagonal_column(rows[1:2, :])
    live_cols = diagonal_column(rows[2:3, :])
    same = owner_col == owner_row
    slot_row = jnp.sum(jnp.where(same & (sub < lane), 1, 0), axis=0, keepdims=True)
    slot_col = jnp.sum(jnp.where(same & (lane < sub), 1, 0), axis=1, keepdims=True)
    owned = owner_col == lane
    for slot in range(2):
        hit = owned & (slot_col == slot)
        for row, value in ((slot, sub), (2 + slot, live_rows), (4 + slot, live_cols)):
            table[row : row + 1, :] = jnp.sum(jnp.where(hit, value, 0), axis=0, keepdims=True)
    table[6:7, :] = owner_row
    table[7:8, :] = slot_row


def kernel(
    grads, map_ref, dims_ref, left, right, out_ref,
    g, gin, pair, rsin, red, out1, in1, lv, rv, g32, prod, pin, dsc, xin, y32, out2, in2, f32s, rows, table, tab,
    load_sem, core_s, core_r, rs_s, rs_r, red_s, red_r, a1_s, a1_r, e_s, e_r, x_s, x_r, a2_s, a2_r,
):
    me = lax.axis_index("owner")
    dp = lax.axis_index("dp")
    x, z = lax.div(me, 8), lax.rem(me, 8)
    y, c = lax.div(dp, 2), lax.rem(dp, 2)
    other = dp + 1 - 2 * c

    load_g = pltpu.make_async_copy(grads, g, load_sem.at[0])
    load_l = pltpu.make_async_copy(left.at[c], lv, load_sem.at[1])
    load_r = pltpu.make_async_copy(right.at[c], rv, load_sem.at[2])
    load_g.start()

    def owner_at(i):
        return lax.rem(x + lax.rem(i, 8), 8) * 8 + lax.rem(z + lax.div(i, 8), 8)

    def dp_at(offset):
        return lax.rem(y + offset, NY)

    barrier = pltpu.get_barrier_semaphore()
    signal(barrier, me, other)
    for offset in FAR_FIRST:
        signal(barrier, me, dp_at(offset) * 2 + c)

    def greet(i, carry):
        signal(barrier, owner_at(i), dp)
        return carry

    lax.fori_loop(1, NO, greet, 0)
    pl.semaphore_wait(barrier, 1 + 7 + NO - 1)

    mine, theirs = c * HALF, (1 - c) * HALF
    load_g.wait()
    halves = []
    for i, offset in enumerate(FAR_FIRST + (0,)):
        tile = pl.ds(pl.multiple_of(dp_at(offset) * LANES, LANES), LANES)
        copy = remote(g.at[pl.ds(theirs, HALF), :, tile], gin.at[i], core_s.at[i], core_r.at[i], me, other)
        copy.start()
        halves.append((copy, tile))
    load_l.start()
    load_r.start()
    sends = []
    for i, offset in enumerate(FAR_FIRST):
        copy, tile = halves[i]
        copy.wait_recv()

        def add(b, carry, i=i, tile=tile):
            pair[i, b] = (g[mine + b, :, tile].astype(F32) + gin[i, b].astype(F32)).astype(BF16)
            return carry

        lax.fori_loop(0, HALF, add, 0, unroll=4)
        send = remote(pair.at[i], rsin.at[i], rs_s.at[i], rs_r.at[i], me, dp_at(offset) * 2 + c)
        send.start()
        sends.append(send)

    build_tables(map_ref, dims_ref, rows, table)
    to_scalars = pltpu.make_async_copy(table, tab, load_sem.at[3])
    to_scalars.start()
    to_scalars.wait()

    own_copy, own_tile = halves[7]
    own_copy.wait_recv()
    for send in sends:
        send.wait_recv()

    def total(b, carry):
        acc = g[mine + b, :, own_tile].astype(F32) + gin[7, b].astype(F32)
        for i in range(7):
            acc = acc + rsin[i, b].astype(F32)
        red[mine + b] = acc.astype(BF16)
        return carry

    lax.fori_loop(0, HALF, total, 0, unroll=2)
    share = remote(red.at[pl.ds(mine, HALF)], red.at[pl.ds(mine, HALF)], red_s, red_r, me, other)
    share.start()
    share.wait_recv()

    def block_at(t):
        return jnp.clip(tab[c, t], 0, NB - 1)

    in1[me] = red[block_at(me)]

    def dispatch(i, carry):
        t = owner_at(i)
        out1[t] = red[block_at(t)]
        remote(out1.at[t], in1.at[me], a1_s, a1_r, t, dp).start()
        return carry

    lax.fori_loop(1, NO, dispatch, 0)
    load_l.wait()
    pltpu.make_async_copy(out1.at[pl.ds(0, NO - 1)], in1.at[pl.ds(0, NO - 1)], a1_r).wait()

    live_rows, live_cols = tab[2 + c, me], tab[4 + c, me]
    in_columns = jnp.where(y < live_cols, 1, 0)
    row_limit = live_rows * 2 * in_columns

    def place(q, carry):
        tile = in1[q].astype(F32)
        keep = lax.broadcasted_iota(I32, (16, LANES), 0) < row_limit
        g32[pl.ds(q, 16, stride=NO), :] = jnp.where(keep, tile, 0.0)
        return carry

    lax.fori_loop(0, NO, place, 0, unroll=4)
    product = jnp.dot(lv[...], g32[pl.ds(0, 8 * LANES), :].astype(BF16), preferred_element_type=F32).astype(BF16)
    prod[...] = product.reshape(NY, LANES, LANES)

    my_tile = pl.ds(pl.multiple_of(y * LANES, LANES), LANES)
    bands = []
    for i, offset in enumerate(FAR_FIRST):
        t = dp_at(offset)
        copy = remote(prod.at[t], pin.at[:, my_tile], e_s.at[i], e_r.at[i], me, t * 2 + c)
        copy.start()
        bands.append(copy)
    pin[:, my_tile] = prod[y]
    load_r.wait()
    for copy in bands:
        copy.wait_recv()
    update = jnp.dot(pin[...], rv[...], preferred_element_type=F32)
    column_limit = live_cols * LANES * jnp.where(y < live_rows, 1, 0)
    keep = lax.broadcasted_iota(I32, (LANES, 8 * LANES), 1) < column_limit
    update = jnp.where(keep, update, 0.0).astype(BF16)
    for half in range(2):
        for j in range(8):
            dsc[half, j] = update[half * NO : (half + 1) * NO, j * LANES : (j + 1) * LANES]
    swap = remote(dsc.at[1 - c], xin, x_s, x_r, me, other)
    swap.start()
    for j in range(8):
        y32[pl.ds(c * 8 + j, NO, stride=16), :] = dsc[c, j].astype(F32)
    swap.wait_recv()
    for j in range(8):
        y32[pl.ds((1 - c) * 8 + j, NO, stride=16), :] = xin[j].astype(F32)
    out2[...] = y32[pl.ds(0, NO * 16), :].astype(BF16).reshape(NO, 16, LANES)

    in2[me] = out2[me]

    def give_back(i, carry):
        t = owner_at(i)
        remote(out2.at[t], in2.at[me], a2_s, a2_r, t, dp).start()
        return carry

    lax.fori_loop(1, NO, give_back, 0)
    pltpu.make_async_copy(out2.at[pl.ds(0, NO - 1)], in2.at[pl.ds(0, NO - 1)], a2_r).wait()

    def pick(b, carry):
        both = in2[jnp.clip(tab[6, b], 0, NO - 1)].astype(F32)
        first = jnp.where(tab[7, b] == 0, 1, 0)
        chosen = jnp.where(first == 1, both[:8], both[8:])
        f32s[pl.ds(pl.multiple_of(b * 8, 8), 8), :] = chosen
        return carry

    lax.fori_loop(0, NB, pick, 0, unroll=4)
    for j in range(8):
        out_ref[:, j * LANES : (j + 1) * LANES] = f32s[pl.ds(j, NB, stride=8), :].astype(BF16)

    for copy, _ in halves:
        copy.wait_send()
    for copy in sends:
        copy.wait_send()
    share.wait_send()
    pltpu.make_async_copy(out1.at[pl.ds(0, NO - 1)], in1.at[pl.ds(0, NO - 1)], a1_s).wait()
    for copy in bands:
        copy.wait_send()
    swap.wait_send()
    pltpu.make_async_copy(out2.at[pl.ds(0, NO - 1)], in2.at[pl.ds(0, NO - 1)], a2_s).wait()


def on_device(grads, owner_map, block_dims, left_root, right_root):
    any_spec = pl.BlockSpec(memory_space=pltpu.HBM)
    vmem_spec = pl.BlockSpec(memory_space=pltpu.VMEM)
    dma = pltpu.SemaphoreType.DMA
    out = pl.pallas_call(
        kernel,
        out_shape=jax.ShapeDtypeStruct((NB, 8 * LANES), BF16),
        in_specs=[any_spec, vmem_spec, vmem_spec, any_spec, any_spec],
        out_specs=vmem_spec,
        scratch_shapes=[
            pltpu.VMEM((NB, 16, 8 * LANES), BF16),
            pltpu.VMEM((8, HALF, 16, LANES), BF16),
            pltpu.VMEM((7, HALF, 16, LANES), BF16),
            pltpu.VMEM((7, HALF, 16, LANES), BF16),
            pltpu.VMEM((NB, 16, LANES), BF16),
            pltpu.VMEM((NO, 16, LANES), BF16),
            pltpu.VMEM((NO, 16, LANES), BF16),
            pltpu.VMEM((8 * LANES, 8 * LANES), BF16),
            pltpu.VMEM((8 * LANES, 8 * LANES), BF16),
            pltpu.VMEM((8 * LANES + NO, LANES), F32),
            pltpu.VMEM((NY, LANES, LANES), BF16),
            pltpu.VMEM((LANES, 8 * LANES), BF16),
            pltpu.VMEM((2, 8, NO, LANES), BF16),
            pltpu.VMEM((8, NO, LANES), BF16),
            pltpu.VMEM((NO * 16 + 16, LANES), F32),
            pltpu.VMEM((NO, 16, LANES), BF16),
            pltpu.VMEM((NO, 16, LANES), BF16),
            pltpu.VMEM((NB * 8 + 8, LANES), F32),
            pltpu.VMEM((8, LANES), I32),
            pltpu.VMEM((8, LANES), I32),
            pltpu.SMEM((8, LANES), I32),
            dma((4,)),
            dma((8,)), dma((8,)),
            dma((7,)), dma((7,)),
            dma, dma,
            dma, dma,
            dma((7,)), dma((7,)),
            dma, dma,
            dma, dma,
        ],
        compiler_params=pltpu.CompilerParams(
            collective_id=0, has_side_effects=True, vmem_limit_bytes=60 * 1024 * 1024
        ),
    )(
        grads.reshape(NB, 16, 8 * LANES),
        owner_map.reshape(1, NB),
        block_dims.T,
        left_root[0],
        right_root[0],
    )
    return out.reshape(NB, 1, 1, 8 * LANES)


def solution(mesh):
    placed = (
        P("dp", None, None, "owner", None),
        P(),
        P(),
        P("owner", None, None, None),
        P("owner", None, None, None),
    )
    return jax.shard_map(
        on_device,
        mesh=mesh,
        in_specs=placed,
        out_specs=P(None, "dp", "owner", None),
        check_vma=False,
    )
```

time: 199 us -> 82.6 us (0.42)
  waiting for transfers between devices: 133 us -> 0 us
  Pallas kernels: 0 us -> 80.9 us
  blocking collectives: 26.7 us -> 0 us
  between operations: 13.5 us -> 0.01 us
  starting transfers between devices: 11.1 us -> 0 us
  matrix products: 7.12 us -> 0 us
  other arithmetic: 5.34 us -> 0 us
    pallas_call x0 -> x1, Pallas kernels: none -> 80.9 us  [on_device(): pl.pallas_call(kernel, out_shape=jax.ShapeDtypeStruct((NB, 8 * LANES), BF...]
    reduce_scatter x1 -> x0, waiting for transfers between devices: 77.5 us -> none  [on_device(): lax.psum_scatter(replica_terms, 'dp', scatter_dimension=1, tiled=True)]
    all_gather x1 -> x0, waiting for transfers between devices: 42.7 us -> none  [on_device(): lax.all_gather(masked, 'dp', axis=1, tiled=True)]
    all_to_all x1 -> x0, blocking collectives: 26.7 us -> none  [on_device(): lax.all_to_all(update, 'owner', split_axis=1, concat_axis=1, tiled=True)]
    all_to_all x1 -> x0, waiting for transfers between devices: 12.3 us -> none  [on_device(): lax.all_to_all(outgoing, 'owner', split_axis=1, concat_axis=1, tiled=True)]
    all_to_all x1 -> x0, starting transfers between devices: 11.1 us -> none  [on_device(): lax.all_to_all(outgoing, 'owner', split_axis=1, concat_axis=1, tiled=True)]
    dot_general x3 -> x0, matrix products: 7.12 us -> none  [the longest x1 5.12 us: on_device(): jnp.einsum('csk,ckn->csn', product_rows, right_full, preferred_element_ty...]
    convert_element_type x1 -> x0, other arithmetic: 4 us -> none  [on_device(): replica_terms = grads[0].astype(jnp.float32)]
  transfers between devices with their start and end apart: 3 -> 0, of which waited for: 3 -> 0; matrix products, arithmetic and copies ran while one was open for 0% -> 0% of each run, Pallas kernels for 0% -> 0%
where the time goes in v1:
time: 82.6 us; the launch traced here: 82.4 us
  Pallas kernels  80.9 us (98%)
  local copies, waits for them, and re-layouts  1.54 us (2%)
    pallas_call x1, Pallas kernels, on_device(): pl.pallas_call(kernel, out_shape=jax.ShapeDtypeStruct((NB, 8 * LANES), BF...  80.9 us

profile of v1, /device:TPU:1, one launch (start us, length us, event | category | flops | bytes accessed | tf_op | source)
XLA Modules:
  0.0 82.4 jit_solution(16014609483627764933)
XLA Ops:
  0.0 80.9 %shard_map.55 = bf16[48,1024]{1,0:T(8,128)(2,1)} custom-call(bf16[48,16,1024]{2,1,0:T(8,128)(2,1)} %bitcast.8, s32[1,48]{1,0:T(1,128)} %bitcast.11, s32[2,48]{1,0:T(2,128)} %bitcast.10, bf16[2,1024,1024]{2,1,0:T(8,128)(2,1)} %bitcast.6, bf16[2,1024,1024]{2,1,0:T(8,128)(2,1)} %bitcast.7), custom_call_target="tpu_custom_call" | custom-call | tf_op jit(solution)/shard_map/pallas_call | solution.py:232
  80.9 1.5 %copy.7 = bf16[48,1,1,1024]{3,0,2,1:T(8,128)(2,1)} copy(bf16[48,1,1,1024]{3,0,2,1:T(8,128)(2,1)} %bitcast.9) | data formatting | bytes 196608

commit v2 on v1

--- a/solution.py
+++ b/solution.py
@@ -11,10 +11,12 @@
 F32, BF16, I32 = jnp.float32, jnp.bfloat16, jnp.int32
 NB = 48
 HALF = NB // 2
+QUARTER = HALF // 2
 NO = 64
 NY = 8
 LANES = 128
 FAR_FIRST = (4, 3, 5, 2, 6, 1, 7)
+TILE_ORDER = (4, 3, 5, 1, 7, 2, 6, 0)
 
 
 def remote(src, dst, send_sem, recv_sem, owner, dp):
@@ -58,8 +60,8 @@
 
 def kernel(
     grads, map_ref, dims_ref, left, right, out_ref,
-    g, gin, pair, rsin, red, out1, in1, lv, rv, g32, prod, pin, dsc, xin, y32, out2, in2, f32s, rows, table, tab,
-    load_sem, core_s, core_r, rs_s, rs_r, red_s, red_r, a1_s, a1_r, e_s, e_r, x_s, x_r, a2_s, a2_r,
+    g, gin, pair, far, mid, near, relayed, red, out1, in1, lv, rv, g32, prod, pin, dsc, xin, y32, out2, in2, f32s, rows, table, tab,
+    load_sem, plane, core_s, core_r, rs_s, rs_r, red_s, red_r, a1_s, a1_r, e_s, e_r, x_s, x_r, a2_s, a2_r,
 ):
     me = lax.axis_index("owner")
     dp = lax.axis_index("dp")
@@ -72,69 +74,115 @@
     load_r = pltpu.make_async_copy(right.at[c], rv, load_sem.at[2])
     load_g.start()
 
+    def along_x(i):
+        return lax.rem(x + i, 8) * 8 + z
+
+    def along_z(i):
+        return x * 8 + lax.rem(z + i, 8)
+
     def owner_at(i):
         return lax.rem(x + lax.rem(i, 8), 8) * 8 + lax.rem(z + lax.div(i, 8), 8)
 
     def dp_at(offset):
         return lax.rem(y + offset, NY)
 
+    pending = []
     barrier = pltpu.get_barrier_semaphore()
     signal(barrier, me, other)
-    for offset in FAR_FIRST:
+    for offset in (1, 7, 2, 6):
         signal(barrier, me, dp_at(offset) * 2 + c)
-
-    def greet(i, carry):
-        signal(barrier, owner_at(i), dp)
-        return carry
-
-    lax.fori_loop(1, NO, greet, 0)
-    pl.semaphore_wait(barrier, 1 + 7 + NO - 1)
+    for i in range(1, 8):
+        signal(barrier, along_x(i), dp)
+        signal(barrier, along_z(i), dp)
+    pl.semaphore_wait(barrier, 1 + 4 + 14)
 
     mine, theirs = c * HALF, (1 - c) * HALF
     load_g.wait()
-    halves = []
-    for i, offset in enumerate(FAR_FIRST + (0,)):
+    halves = {}
+    for offset in TILE_ORDER:
         tile = pl.ds(pl.multiple_of(dp_at(offset) * LANES, LANES), LANES)
-        copy = remote(g.at[pl.ds(theirs, HALF), :, tile], gin.at[i], core_s.at[i], core_r.at[i], me, other)
+        copy = remote(
+            g.at[pl.ds(theirs, HALF), :, tile], gin.at[offset], core_s.at[offset], core_r.at[offset], me, other
+        )
         copy.start()
-        halves.append((copy, tile))
+        pending.append(copy.wait_send)
+        halves[offset] = (copy, tile)
     load_l.start()
     load_r.start()
-    sends = []
-    for i, offset in enumerate(FAR_FIRST):
-        copy, tile = halves[i]
-        copy.wait_recv()
-
-        def add(b, carry, i=i, tile=tile):
-            pair[i, b] = (g[mine + b, :, tile].astype(F32) + gin[i, b].astype(F32)).astype(BF16)
+
+    def core_sum(offset, b):
+        return g[mine + b, :, halves[offset][1]].astype(F32) + gin[offset, b].astype(F32)
+
+    def send_sum(offset, hops):
+        halves[offset][0].wait_recv()
+
+        def add(b, carry):
+            pair[offset, b] = core_sum(offset, b).astype(BF16)
             return carry
 
         lax.fori_loop(0, HALF, add, 0, unroll=4)
-        send = remote(pair.at[i], rsin.at[i], rs_s.at[i], rs_r.at[i], me, dp_at(offset) * 2 + c)
-        send.start()
-        sends.append(send)
+        copies = []
+        for buffer, index, first, count, target, k in hops:
+            copy = remote(
+                pair.at[offset, pl.ds(first, count)], buffer.at[index], rs_s.at[k], rs_r.at[k], me, dp_at(target) * 2 + c
+            )
+            copy.start()
+            pending.append(copy.wait_send)
+            copies.append(copy)
+        return copies
+
+    far_up, far_down = send_sum(4, ((far, 0, 0, QUARTER, 2, 0), (far, 1, QUARTER, QUARTER, 6, 1)))
+    (mid_up,) = send_sum(3, ((mid, 0, 0, HALF, 1, 2),))
+    (mid_down,) = send_sum(5, ((mid, 1, 0, HALF, 7, 3),))
+    (near_up,) = send_sum(1, ((near, 0, 0, HALF, 1, 4),))
+    (near_down,) = send_sum(7, ((near, 1, 0, HALF, 7, 5),))
+    for i in range(1, 8):
+        signal(plane, along_x(i), dp)
+    relays = []
+    for way, offset, first, arrivals in ((0, 2, 0, (far_up, mid_up)), (1, 6, QUARTER, (far_down, mid_down))):
+        halves[offset][0].wait_recv()
+        for copy in arrivals:
+            copy.wait_recv()
+
+        def relay_both(b, carry, way=way, offset=offset, first=first):
+            acc = core_sum(offset, first + b) + mid[way, first + b].astype(F32) + far[way, b].astype(F32)
+            pair[offset, first + b] = acc.astype(BF16)
+            return carry
+
+        def relay_one(b, carry, way=way, offset=offset, first=QUARTER - first):
+            pair[offset, first + b] = (core_sum(offset, first + b) + mid[way, first + b].astype(F32)).astype(BF16)
+            return carry
+
+        lax.fori_loop(0, QUARTER, relay_both, 0, unroll=4)
+        lax.fori_loop(0, QUARTER, relay_one, 0, unroll=4)
+        copy = remote(pair.at[offset], relayed.at[way], rs_s.at[6 + way], rs_r.at[6 + way], me, dp_at(offset) * 2 + c)
+        copy.start()
+        pending.append(copy.wait_send)
+        relays.append(copy)
 
     build_tables(map_ref, dims_ref, rows, table)
     to_scalars = pltpu.make_async_copy(table, tab, load_sem.at[3])
     to_scalars.start()
     to_scalars.wait()
 
-    own_copy, own_tile = halves[7]
-    own_copy.wait_recv()
-    for send in sends:
-        send.wait_recv()
+    halves[0][0].wait_recv()
+    for copy in (near_up, near_down, *relays):
+        copy.wait_recv()
 
     def total(b, carry):
-        acc = g[mine + b, :, own_tile].astype(F32) + gin[7, b].astype(F32)
-        for i in range(7):
-            acc = acc + rsin[i, b].astype(F32)
+        acc = core_sum(0, b)
+        for way in range(2):
+            acc = acc + near[way, b].astype(F32) + relayed[way, b].astype(F32)
         red[mine + b] = acc.astype(BF16)
         return carry
 
-    lax.fori_loop(0, HALF, total, 0, unroll=2)
+    lax.fori_loop(0, HALF, total, 0, unroll=4)
     share = remote(red.at[pl.ds(mine, HALF)], red.at[pl.ds(mine, HALF)], red_s, red_r, me, other)
     share.start()
+    pending.append(share.wait_send)
     share.wait_recv()
+
+    pl.semaphore_wait(plane, 7)
 
     def block_at(t):
         return jnp.clip(tab[c, t], 0, NB - 1)
@@ -148,6 +196,7 @@
         return carry
 
     lax.fori_loop(1, NO, dispatch, 0)
+    pending.append(pltpu.make_async_copy(out1.at[pl.ds(0, NO - 1)], in1.at[pl.ds(0, NO - 1)], a1_s).wait)
     load_l.wait()
     pltpu.make_async_copy(out1.at[pl.ds(0, NO - 1)], in1.at[pl.ds(0, NO - 1)], a1_r).wait()
 
@@ -171,6 +220,7 @@
         t = dp_at(offset)
         copy = remote(prod.at[t], pin.at[:, my_tile], e_s.at[i], e_r.at[i], me, t * 2 + c)
         copy.start()
+        pending.append(copy.wait_send)
         bands.append(copy)
     pin[:, my_tile] = prod[y]
     load_r.wait()
@@ -185,6 +235,7 @@
             dsc[half, j] = update[half * NO : (half + 1) * NO, j * LANES : (j + 1) * LANES]
     swap = remote(dsc.at[1 - c], xin, x_s, x_r, me, other)
     swap.start()
+    pending.append(swap.wait_send)
     for j in range(8):
         y32[pl.ds(c * 8 + j, NO, stride=16), :] = dsc[c, j].astype(F32)
     swap.wait_recv()
@@ -200,6 +251,7 @@
         return carry
 
     lax.fori_loop(1, NO, give_back, 0)
+    pending.append(pltpu.make_async_copy(out2.at[pl.ds(0, NO - 1)], in2.at[pl.ds(0, NO - 1)], a2_s).wait)
     pltpu.make_async_copy(out2.at[pl.ds(0, NO - 1)], in2.at[pl.ds(0, NO - 1)], a2_r).wait()
 
     def pick(b, carry):
@@ -213,16 +265,8 @@
     for j in range(8):
         out_ref[:, j * LANES : (j + 1) * LANES] = f32s[pl.ds(j, NB, stride=8), :].astype(BF16)
 
-    for copy, _ in halves:
-        copy.wait_send()
-    for copy in sends:
-        copy.wait_send()
-    share.wait_send()
-    pltpu.make_async_copy(out1.at[pl.ds(0, NO - 1)], in1.at[pl.ds(0, NO - 1)], a1_s).wait()
-    for copy in bands:
-        copy.wait_send()
-    swap.wait_send()
-    pltpu.make_async_copy(out2.at[pl.ds(0, NO - 1)], in2.at[pl.ds(0, NO - 1)], a2_s).wait()
+    for wait in pending:
+        wait()
 
 
 def on_device(grads, owner_map, block_dims, left_root, right_root):
@@ -237,8 +281,11 @@
         scratch_shapes=[
             pltpu.VMEM((NB, 16, 8 * LANES), BF16),
             pltpu.VMEM((8, HALF, 16, LANES), BF16),
-            pltpu.VMEM((7, HALF, 16, LANES), BF16),
-            pltpu.VMEM((7, HALF, 16, LANES), BF16),
+            pltpu.VMEM((8, HALF, 16, LANES), BF16),
+            pltpu.VMEM((2, QUARTER, 16, LANES), BF16),
+            pltpu.VMEM((2, HALF, 16, LANES), BF16),
+            pltpu.VMEM((2, HALF, 16, LANES), BF16),
+            pltpu.VMEM((2, HALF, 16, LANES), BF16),
             pltpu.VMEM((NB, 16, LANES), BF16),
             pltpu.VMEM((NO, 16, LANES), BF16),
             pltpu.VMEM((NO, 16, LANES), BF16),
@@ -257,8 +304,9 @@
             pltpu.VMEM((8, LANES), I32),
             pltpu.SMEM((8, LANES), I32),
             dma((4,)),
+            pltpu.SemaphoreType.REGULAR,
             dma((8,)), dma((8,)),
-            dma((7,)), dma((7,)),
+            dma((8,)), dma((8,)),
             dma, dma,
             dma, dma,
             dma((7,)), dma((7,)),

time: 82.6 us -> 74.4 us (0.901)
  Pallas kernels: 80.9 us -> 72.7 us
    pallas_call x1, Pallas kernels: 80.9 us -> 72.7 us  [on_device(): pl.pallas_call(kernel, out_shape=jax.ShapeDtypeStruct((NB, 8 * LANES), BF...]
where the time goes in v2:
time: 74.4 us; the launch traced here: 74.3 us
  Pallas kernels  72.7 us (98%)
  local copies, waits for them, and re-layouts  1.54 us (2%)
    pallas_call x1, Pallas kernels, on_device(): pl.pallas_call(kernel, out_shape=jax.ShapeDtypeStruct((NB, 8 * LANES), BF...  72.7 us
    unnamed x1, local copies, waits for them, and re-layouts  1.54 us

profile of v2, /device:TPU:1, one launch (start us, length us, event | category | flops | bytes accessed | tf_op | source)
XLA Modules:
  0.0 74.3 jit_solution(14021061610959612474)
XLA Ops:
  0.0 72.7 %shard_map.55 = bf16[48,1024]{1,0:T(8,128)(2,1)} custom-call(bf16[48,16,1024]{2,1,0:T(8,128)(2,1)} %bitcast.8, s32[1,48]{1,0:T(1,128)} %bitcast.11, s32[2,48]{1,0:T(2,128)} %bitcast.10, bf16[2,1024,1024]{2,1,0:T(8,128)(2,1)} %bitcast.6, bf16[2,1024,1024]{2,1,0:T(8,128)(2,1)} %bitcast.7), custom_call_target="tpu_custom_call" | custom-call | tf_op jit(solution)/shard_map/pallas_call | solution.py:276
  72.7 1.5 %copy.7 = bf16[48,1,1,1024]{3,0,2,1:T(8,128)(2,1)} copy(bf16[48,1,1,1024]{3,0,2,1:T(8,128)(2,1)} %bitcast.9) | data formatting | bytes 196608

commit v3 on v2

--- a/solution.py
+++ b/solution.py
@@ -16,7 +16,7 @@
 NY = 8
 LANES = 128
 FAR_FIRST = (4, 3, 5, 2, 6, 1, 7)
-TILE_ORDER = (4, 3, 5, 1, 7, 2, 6, 0)
+TILE_ORDER = (3, 5, 4, 1, 7, 2, 6, 0)
 
 
 def remote(src, dst, send_sem, recv_sem, owner, dp):
@@ -113,52 +113,53 @@
     def core_sum(offset, b):
         return g[mine + b, :, halves[offset][1]].astype(F32) + gin[offset, b].astype(F32)
 
-    def send_sum(offset, hops):
-        halves[offset][0].wait_recv()
-
+    def sum_blocks(offset, first, count, terms=()):
         def add(b, carry):
-            pair[offset, b] = core_sum(offset, b).astype(BF16)
+            acc = core_sum(offset, first + b)
+            for buffer, way, start in terms:
+                acc = acc + buffer[way, start + b].astype(F32)
+            pair[offset, first + b] = acc.astype(BF16)
             return carry
 
-        lax.fori_loop(0, HALF, add, 0, unroll=4)
-        copies = []
-        for buffer, index, first, count, target, k in hops:
-            copy = remote(
-                pair.at[offset, pl.ds(first, count)], buffer.at[index], rs_s.at[k], rs_r.at[k], me, dp_at(target) * 2 + c
-            )
-            copy.start()
-            pending.append(copy.wait_send)
-            copies.append(copy)
-        return copies
-
-    far_up, far_down = send_sum(4, ((far, 0, 0, QUARTER, 2, 0), (far, 1, QUARTER, QUARTER, 6, 1)))
-    (mid_up,) = send_sum(3, ((mid, 0, 0, HALF, 1, 2),))
-    (mid_down,) = send_sum(5, ((mid, 1, 0, HALF, 7, 3),))
-    (near_up,) = send_sum(1, ((near, 0, 0, HALF, 1, 4),))
-    (near_down,) = send_sum(7, ((near, 1, 0, HALF, 7, 5),))
+        lax.fori_loop(0, count, add, 0, unroll=4)
+
+    def send_sums(offset, first, count, target, buffer, k):
+        copy = remote(
+            pair.at[offset, pl.ds(first, count)], buffer, rs_s.at[k], rs_r.at[k], me, dp_at(target) * 2 + c
+        )
+        copy.start()
+        pending.append(copy.wait_send)
+        return copy
+
+    ways = ((0, 2, 3, 1, 0, QUARTER), (1, 6, 5, 7, QUARTER, 0))
+    arrivals = {}
+    for way, own, three, step, both, alone in ways:
+        halves[three][0].wait_recv()
+        sum_blocks(three, alone, QUARTER)
+        arrivals[way, "alone"] = send_sums(three, alone, QUARTER, step, mid.at[way, pl.ds(alone, QUARTER)], way)
+    halves[4][0].wait_recv()
+    for way, own, three, step, both, alone in ways:
+        sum_blocks(4, both, QUARTER)
+        arrivals[way, "far"] = send_sums(4, both, QUARTER, own, far.at[way], 2 + way)
+    for way, own, three, step, both, alone in ways:
+        sum_blocks(three, both, QUARTER)
+        arrivals[way, "both"] = send_sums(three, both, QUARTER, step, mid.at[way, pl.ds(both, QUARTER)], 4 + way)
+    for way, own, three, step, both, alone in ways:
+        halves[step][0].wait_recv()
+        sum_blocks(step, 0, HALF)
+        arrivals[way, "near"] = send_sums(step, 0, HALF, step, near.at[way], 6 + way)
     for i in range(1, 8):
         signal(plane, along_x(i), dp)
-    relays = []
-    for way, offset, first, arrivals in ((0, 2, 0, (far_up, mid_up)), (1, 6, QUARTER, (far_down, mid_down))):
-        halves[offset][0].wait_recv()
-        for copy in arrivals:
-            copy.wait_recv()
-
-        def relay_both(b, carry, way=way, offset=offset, first=first):
-            acc = core_sum(offset, first + b) + mid[way, first + b].astype(F32) + far[way, b].astype(F32)
-            pair[offset, first + b] = acc.astype(BF16)
-            return carry
-
-        def relay_one(b, carry, way=way, offset=offset, first=QUARTER - first):
-            pair[offset, first + b] = (core_sum(offset, first + b) + mid[way, first + b].astype(F32)).astype(BF16)
-            return carry
-
-        lax.fori_loop(0, QUARTER, relay_both, 0, unroll=4)
-        lax.fori_loop(0, QUARTER, relay_one, 0, unroll=4)
-        copy = remote(pair.at[offset], relayed.at[way], rs_s.at[6 + way], rs_r.at[6 + way], me, dp_at(offset) * 2 + c)
-        copy.start()
-        pending.append(copy.wait_send)
-        relays.append(copy)
+    for way, own, three, step, both, alone in ways:
+        halves[own][0].wait_recv()
+        arrivals[way, "alone"].wait_recv()
+        sum_blocks(own, alone, QUARTER, ((mid, way, alone),))
+        arrivals[way, "first"] = send_sums(own, alone, QUARTER, own, relayed.at[way, pl.ds(alone, QUARTER)], 8 + way)
+    for way, own, three, step, both, alone in ways:
+        arrivals[way, "far"].wait_recv()
+        arrivals[way, "both"].wait_recv()
+        sum_blocks(own, both, QUARTER, ((mid, way, both), (far, way, 0)))
+        arrivals[way, "last"] = send_sums(own, both, QUARTER, own, relayed.at[way, pl.ds(both, QUARTER)], 10 + way)
 
     build_tables(map_ref, dims_ref, rows, table)
     to_scalars = pltpu.make_async_copy(table, tab, load_sem.at[3])
@@ -166,8 +167,9 @@
     to_scalars.wait()
 
     halves[0][0].wait_recv()
-    for copy in (near_up, near_down, *relays):
-        copy.wait_recv()
+    for way in range(2):
+        for part in ("near", "first", "last"):
+            arrivals[way, part].wait_recv()
 
     def total(b, carry):
         acc = core_sum(0, b)
@@ -306,7 +308,7 @@
             dma((4,)),
             pltpu.SemaphoreType.REGULAR,
             dma((8,)), dma((8,)),
-            dma((8,)), dma((8,)),
+            dma((12,)), dma((12,)),
             dma, dma,
             dma, dma,
             dma((7,)), dma((7,)),

time: 74.4 us -> 73.6 us (0.989)
  Pallas kernels: 72.7 us -> 71.8 us
    pallas_call x1, Pallas kernels: 72.7 us -> 71.8 us  [on_device(): pl.pallas_call(kernel, out_shape=jax.ShapeDtypeStruct((NB, 8 * LANES), BF...]
where the time goes in v3:
time: 73.6 us; the launch traced here: 73.4 us
  Pallas kernels  71.8 us (98%)
  local copies, waits for them, and re-layouts  1.54 us (2%)
    pallas_call x1, Pallas kernels, on_device(): pl.pallas_call(kernel, out_shape=jax.ShapeDtypeStruct((NB, 8 * LANES), BF...  71.8 us
    unnamed x1, local copies, waits for them, and re-layouts  1.54 us

profile of v3, /device:TPU:1, one launch (start us, length us, event | category | flops | bytes accessed | tf_op | source)
XLA Modules:
  0.0 73.4 jit_solution(3253259312808090964)
XLA Ops:
  0.0 71.8 %shard_map.55 = bf16[48,1024]{1,0:T(8,128)(2,1)} custom-call(bf16[48,16,1024]{2,1,0:T(8,128)(2,1)} %bitcast.8, s32[1,48]{1,0:T(1,128)} %bitcast.11, s32[2,48]{1,0:T(2,128)} %bitcast.10, bf16[2,1024,1024]{2,1,0:T(8,128)(2,1)} %bitcast.6, bf16[2,1024,1024]{2,1,0:T(8,128)(2,1)} %bitcast.7), custom_call_target="tpu_custom_call" | custom-call | tf_op jit(solution)/shard_map/pallas_call | solution.py:278
  71.8 1.5 %copy.7 = bf16[48,1,1,1024]{3,0,2,1:T(8,128)(2,1)} copy(bf16[48,1,1,1024]{3,0,2,1:T(8,128)(2,1)} %bitcast.9) | data formatting | bytes 196608

commit v4 on v3

--- a/solution.py
+++ b/solution.py
@@ -74,11 +74,8 @@
     load_r = pltpu.make_async_copy(right.at[c], rv, load_sem.at[2])
     load_g.start()
 
-    def along_x(i):
-        return lax.rem(x + i, 8) * 8 + z
-
-    def along_z(i):
-        return x * 8 + lax.rem(z + i, 8)
+    def in_line(i):
+        return lax.rem(x + i * c, 8) * 8 + lax.rem(z + i * (1 - c), 8)
 
     def owner_at(i):
         return lax.rem(x + lax.rem(i, 8), 8) * 8 + lax.rem(z + lax.div(i, 8), 8)
@@ -92,9 +89,8 @@
     for offset in (1, 7, 2, 6):
         signal(barrier, me, dp_at(offset) * 2 + c)
     for i in range(1, 8):
-        signal(barrier, along_x(i), dp)
-        signal(barrier, along_z(i), dp)
-    pl.semaphore_wait(barrier, 1 + 4 + 14)
+        signal(barrier, in_line(i), dp)
+    pl.semaphore_wait(barrier, 1 + 4 + 7)
 
     mine, theirs = c * HALF, (1 - c) * HALF
     load_g.wait()
@@ -109,6 +105,7 @@
         halves[offset] = (copy, tile)
     load_l.start()
     load_r.start()
+    signal(plane.at[0], me, other)
 
     def core_sum(offset, b):
         return g[mine + b, :, halves[offset][1]].astype(F32) + gin[offset, b].astype(F32)
@@ -148,8 +145,9 @@
         halves[step][0].wait_recv()
         sum_blocks(step, 0, HALF)
         arrivals[way, "near"] = send_sums(step, 0, HALF, step, near.at[way], 6 + way)
+    pl.semaphore_wait(plane.at[0], 1)
     for i in range(1, 8):
-        signal(plane, along_x(i), dp)
+        signal(plane.at[1], in_line(i), dp)
     for way, own, three, step, both, alone in ways:
         halves[own][0].wait_recv()
         arrivals[way, "alone"].wait_recv()
@@ -161,6 +159,8 @@
         sum_blocks(own, both, QUARTER, ((mid, way, both), (far, way, 0)))
         arrivals[way, "last"] = send_sums(own, both, QUARTER, own, relayed.at[way, pl.ds(both, QUARTER)], 10 + way)
 
+    pl.semaphore_wait(plane.at[1], 7)
+    signal(plane.at[2], me, other)
     build_tables(map_ref, dims_ref, rows, table)
     to_scalars = pltpu.make_async_copy(table, tab, load_sem.at[3])
     to_scalars.start()
@@ -184,7 +184,7 @@
     pending.append(share.wait_send)
     share.wait_recv()
 
-    pl.semaphore_wait(plane, 7)
+    pl.semaphore_wait(plane.at[2], 1)
 
     def block_at(t):
         return jnp.clip(tab[c, t], 0, NB - 1)
@@ -213,33 +213,42 @@
         return carry
 
     lax.fori_loop(0, NO, place, 0, unroll=4)
-    product = jnp.dot(lv[...], g32[pl.ds(0, 8 * LANES), :].astype(BF16), preferred_element_type=F32).astype(BF16)
-    prod[...] = product.reshape(NY, LANES, LANES)
+    masked = g32[pl.ds(0, 8 * LANES), :].astype(BF16)
 
     my_tile = pl.ds(pl.multiple_of(y * LANES, LANES), LANES)
+
+    def band(t):
+        rows_of_band = lv[pl.ds(pl.multiple_of(t * LANES, LANES), LANES), :]
+        return jnp.dot(rows_of_band, masked, preferred_element_type=F32).astype(BF16)
+
     bands = []
     for i, offset in enumerate(FAR_FIRST):
         t = dp_at(offset)
-        copy = remote(prod.at[t], pin.at[:, my_tile], e_s.at[i], e_r.at[i], me, t * 2 + c)
+        prod[i] = band(t)
+        copy = remote(prod.at[i], pin.at[:, my_tile], e_s.at[i], e_r.at[i], me, t * 2 + c)
         copy.start()
         pending.append(copy.wait_send)
         bands.append(copy)
-    pin[:, my_tile] = prod[y]
+    pin[:, my_tile] = band(y)
     load_r.wait()
     for copy in bands:
         copy.wait_recv()
-    update = jnp.dot(pin[...], rv[...], preferred_element_type=F32)
     column_limit = live_cols * LANES * jnp.where(y < live_rows, 1, 0)
-    keep = lax.broadcasted_iota(I32, (LANES, 8 * LANES), 1) < column_limit
-    update = jnp.where(keep, update, 0.0).astype(BF16)
-    for half in range(2):
-        for j in range(8):
-            dsc[half, j] = update[half * NO : (half + 1) * NO, j * LANES : (j + 1) * LANES]
-    swap = remote(dsc.at[1 - c], xin, x_s, x_r, me, other)
+    keep = lax.broadcasted_iota(I32, (NO, 8 * LANES), 1) < column_limit
+
+    def update(half):
+        rows_of_half = pin[pl.ds(pl.multiple_of(half * NO, NO), NO), :]
+        return jnp.where(keep, jnp.dot(rows_of_half, rv[...], preferred_element_type=F32), 0.0)
+
+    given = update(1 - c).astype(BF16)
+    for j in range(8):
+        dsc[j] = given[:, j * LANES : (j + 1) * LANES]
+    swap = remote(dsc, xin, x_s, x_r, me, other)
     swap.start()
     pending.append(swap.wait_send)
+    kept = update(c)
     for j in range(8):
-        y32[pl.ds(c * 8 + j, NO, stride=16), :] = dsc[c, j].astype(F32)
+        y32[pl.ds(c * 8 + j, NO, stride=16), :] = kept[:, j * LANES : (j + 1) * LANES]
     swap.wait_recv()
     for j in range(8):
         y32[pl.ds((1 - c) * 8 + j, NO, stride=16), :] = xin[j].astype(F32)
@@ -263,7 +272,7 @@
         f32s[pl.ds(pl.multiple_of(b * 8, 8), 8), :] = chosen
         return carry
 
-    lax.fori_loop(0, NB, pick, 0, unroll=4)
+    lax.fori_loop(0, NB, pick, 0, unroll=8)
     for j in range(8):
         out_ref[:, j * LANES : (j + 1) * LANES] = f32s[pl.ds(j, NB, stride=8), :].astype(BF16)
 
@@ -294,9 +303,9 @@
             pltpu.VMEM((8 * LANES, 8 * LANES), BF16),
             pltpu.VMEM((8 * LANES, 8 * LANES), BF16),
             pltpu.VMEM((8 * LANES + NO, LANES), F32),
-            pltpu.VMEM((NY, LANES, LANES), BF16),
+            pltpu.VMEM((NY - 1, LANES, LANES), BF16),
             pltpu.VMEM((LANES, 8 * LANES), BF16),
-            pltpu.VMEM((2, 8, NO, LANES), BF16),
+            pltpu.VMEM((8, NO, LANES), BF16),
             pltpu.VMEM((8, NO, LANES), BF16),
             pltpu.VMEM((NO * 16 + 16, LANES), F32),
             pltpu.VMEM((NO, 16, LANES), BF16),
@@ -306,7 +315,7 @@
             pltpu.VMEM((8, LANES), I32),
             pltpu.SMEM((8, LANES), I32),
             dma((4,)),
-            pltpu.SemaphoreType.REGULAR,
+            pltpu.SemaphoreType.REGULAR((3,)),
             dma((8,)), dma((8,)),
             dma((12,)), dma((12,)),
             dma, dma,

time: 73.6 us -> 71.6 us (0.973)
  Pallas kernels: 71.8 us -> 69.9 us
    pallas_call x1, Pallas kernels: 71.8 us -> 69.9 us  [on_device(): pl.pallas_call(kernel, out_shape=jax.ShapeDtypeStruct((NB, 8 * LANES), BF...]
where the time goes in v4:
time: 71.6 us; the launch traced here: 71.5 us
  Pallas kernels  69.9 us (98%)
  local copies, waits for them, and re-layouts  1.54 us (2%)
    pallas_call x1, Pallas kernels, on_device(): pl.pallas_call(kernel, out_shape=jax.ShapeDtypeStruct((NB, 8 * LANES), BF...  69.9 us
    unnamed x1, local copies, waits for them, and re-layouts  1.54 us

profile of v4, /device:TPU:1, one launch (start us, length us, event | category | flops | bytes accessed | tf_op | source)
XLA Modules:
  0.0 71.5 jit_solution(13604321029539270242)
XLA Ops:
  0.0 69.9 %shard_map.55 = bf16[48,1024]{1,0:T(8,128)(2,1)} custom-call(bf16[48,16,1024]{2,1,0:T(8,128)(2,1)} %bitcast.8, s32[1,48]{1,0:T(1,128)} %bitcast.11, s32[2,48]{1,0:T(2,128)} %bitcast.10, bf16[2,1024,1024]{2,1,0:T(8,128)(2,1)} %bitcast.6, bf16[2,1024,1024]{2,1,0:T(8,128)(2,1)} %bitcast.7), custom_call_target="tpu_custom_call" | custom-call | tf_op jit(solution)/shard_map/pallas_call | solution.py:287
  69.9 1.5 %copy.7 = bf16[48,1,1,1024]{3,0,2,1:T(8,128)(2,1)} copy(bf16[48,1,1,1024]{3,0,2,1:T(8,128)(2,1)} %bitcast.9) | data formatting | bytes 196608

commit v5 on v4

--- a/solution.py
+++ b/solution.py
@@ -77,8 +77,11 @@
     def in_line(i):
         return lax.rem(x + i * c, 8) * 8 + lax.rem(z + i * (1 - c), 8)
 
+    def far_first(i):
+        return 4 + lax.div(i + 1, 2) * (1 - 2 * lax.rem(i, 2))
+
     def owner_at(i):
-        return lax.rem(x + lax.rem(i, 8), 8) * 8 + lax.rem(z + lax.div(i, 8), 8)
+        return lax.rem(x + far_first(lax.rem(i, 8)), 8) * 8 + lax.rem(z + far_first(lax.div(i, 8)), 8)
 
     def dp_at(offset):
         return lax.rem(y + offset, NY)
@@ -197,7 +200,7 @@
         remote(out1.at[t], in1.at[me], a1_s, a1_r, t, dp).start()
         return carry
 
-    lax.fori_loop(1, NO, dispatch, 0)
+    lax.fori_loop(0, NO - 1, dispatch, 0)
     pending.append(pltpu.make_async_copy(out1.at[pl.ds(0, NO - 1)], in1.at[pl.ds(0, NO - 1)], a1_s).wait)
     load_l.wait()
     pltpu.make_async_copy(out1.at[pl.ds(0, NO - 1)], in1.at[pl.ds(0, NO - 1)], a1_r).wait()
@@ -217,21 +220,29 @@
 
     my_tile = pl.ds(pl.multiple_of(y * LANES, LANES), LANES)
 
-    def band(t):
-        rows_of_band = lv[pl.ds(pl.multiple_of(t * LANES, LANES), LANES), :]
+    def half_band(t, half):
+        rows_of_band = lv[pl.ds(pl.multiple_of(t * LANES + half * NO, NO), NO), :]
         return jnp.dot(rows_of_band, masked, preferred_element_type=F32).astype(BF16)
 
-    bands = []
-    for i, offset in enumerate(FAR_FIRST):
-        t = dp_at(offset)
-        prod[i] = band(t)
-        copy = remote(prod.at[i], pin.at[:, my_tile], e_s.at[i], e_r.at[i], me, t * 2 + c)
-        copy.start()
-        pending.append(copy.wait_send)
-        bands.append(copy)
-    pin[:, my_tile] = band(y)
+    def send_half(part, half):
+        at = pl.ds(pl.multiple_of(half * NO, NO), NO)
+        copies = []
+        for i, offset in enumerate(FAR_FIRST):
+            t = dp_at(offset)
+            prod[part, i] = half_band(t, half)
+            copy = remote(
+                prod.at[part, i], pin.at[at, my_tile], e_s.at[part, i], e_r.at[part, i], me, t * 2 + c
+            )
+            copy.start()
+            pending.append(copy.wait_send)
+            copies.append(copy)
+        pin[at, my_tile] = half_band(y, half)
+        return copies
+
+    theirs_first = send_half(0, 1 - c)
+    mine_next = send_half(1, c)
     load_r.wait()
-    for copy in bands:
+    for copy in theirs_first:
         copy.wait_recv()
     column_limit = live_cols * LANES * jnp.where(y < live_rows, 1, 0)
     keep = lax.broadcasted_iota(I32, (NO, 8 * LANES), 1) < column_limit
@@ -246,6 +257,8 @@
     swap = remote(dsc, xin, x_s, x_r, me, other)
     swap.start()
     pending.append(swap.wait_send)
+    for copy in mine_next:
+        copy.wait_recv()
     kept = update(c)
     for j in range(8):
         y32[pl.ds(c * 8 + j, NO, stride=16), :] = kept[:, j * LANES : (j + 1) * LANES]
@@ -261,7 +274,7 @@
         remote(out2.at[t], in2.at[me], a2_s, a2_r, t, dp).start()
         return carry
 
-    lax.fori_loop(1, NO, give_back, 0)
+    lax.fori_loop(0, NO - 1, give_back, 0)
     pending.append(pltpu.make_async_copy(out2.at[pl.ds(0, NO - 1)], in2.at[pl.ds(0, NO - 1)], a2_s).wait)
     pltpu.make_async_copy(out2.at[pl.ds(0, NO - 1)], in2.at[pl.ds(0, NO - 1)], a2_r).wait()
 
@@ -303,7 +316,7 @@
             pltpu.VMEM((8 * LANES, 8 * LANES), BF16),
             pltpu.VMEM((8 * LANES, 8 * LANES), BF16),
             pltpu.VMEM((8 * LANES + NO, LANES), F32),
-            pltpu.VMEM((NY - 1, LANES, LANES), BF16),
+            pltpu.VMEM((2, NY - 1, NO, LANES), BF16),
             pltpu.VMEM((LANES, 8 * LANES), BF16),
             pltpu.VMEM((8, NO, LANES), BF16),
             pltpu.VMEM((8, NO, LANES), BF16),
@@ -320,7 +333,7 @@
             dma((12,)), dma((12,)),
             dma, dma,
             dma, dma,
-            dma((7,)), dma((7,)),
+            dma((2, 7)), dma((2, 7)),
             dma, dma,
             dma, dma,
         ],

time: 71.6 us -> 69.1 us (0.965)
  Pallas kernels: 69.9 us -> 67.4 us
    pallas_call x1, Pallas kernels: 69.9 us -> 67.4 us  [on_device(): pl.pallas_call(kernel, out_shape=jax.ShapeDtypeStruct((NB, 8 * LANES), BF...]
where the time goes in v5:
time: 69.1 us; the launch traced here: 68.9 us
  Pallas kernels  67.4 us (98%)
  local copies, waits for them, and re-layouts  1.54 us (2%)
    pallas_call x1, Pallas kernels, on_device(): pl.pallas_call(kernel, out_shape=jax.ShapeDtypeStruct((NB, 8 * LANES), BF...  67.4 us
    unnamed x1, local copies, waits for them, and re-layouts  1.54 us

profile of v5, /device:TPU:1, one launch (start us, length us, event | category | flops | bytes accessed | tf_op | source)
XLA Modules:
  0.0 68.9 jit_solution(7992539093244578206)
XLA Ops:
  0.0 67.4 %shard_map.55 = bf16[48,1024]{1,0:T(8,128)(2,1)} custom-call(bf16[48,16,1024]{2,1,0:T(8,128)(2,1)} %bitcast.8, s32[1,48]{1,0:T(1,128)} %bitcast.11, s32[2,48]{1,0:T(2,128)} %bitcast.10, bf16[2,1024,1024]{2,1,0:T(8,128)(2,1)} %bitcast.6, bf16[2,1024,1024]{2,1,0:T(8,128)(2,1)} %bitcast.7), custom_call_target="tpu_custom_call" | custom-call | tf_op jit(solution)/shard_map/pallas_call | solution.py:300
  67.4 1.5 %copy.7 = bf16[48,1,1,1024]{3,0,2,1:T(8,128)(2,1)} copy(bf16[48,1,1,1024]{3,0,2,1:T(8,128)(2,1)} %bitcast.9) | data formatting | bytes 196608

commit v6 on v5

--- a/solution.py
+++ b/solution.py
@@ -69,7 +69,7 @@
     y, c = lax.div(dp, 2), lax.rem(dp, 2)
     other = dp + 1 - 2 * c
 
-    load_g = pltpu.make_async_copy(grads, g, load_sem.at[0])
+    load_g = pltpu.make_async_copy(grads.at[pl.ds(c * HALF, HALF)], g, load_sem.at[0])
     load_l = pltpu.make_async_copy(left.at[c], lv, load_sem.at[1])
     load_r = pltpu.make_async_copy(right.at[c], rv, load_sem.at[2])
     load_g.start()
@@ -96,12 +96,11 @@
     pl.semaphore_wait(barrier, 1 + 4 + 7)
 
     mine, theirs = c * HALF, (1 - c) * HALF
-    load_g.wait()
     halves = {}
     for offset in TILE_ORDER:
         tile = pl.ds(pl.multiple_of(dp_at(offset) * LANES, LANES), LANES)
         copy = remote(
-            g.at[pl.ds(theirs, HALF), :, tile], gin.at[offset], core_s.at[offset], core_r.at[offset], me, other
+            grads.at[pl.ds(theirs, HALF), :, tile], gin.at[offset], core_s.at[offset], core_r.at[offset], me, other
         )
         copy.start()
         pending.append(copy.wait_send)
@@ -111,7 +110,7 @@
     signal(plane.at[0], me, other)
 
     def core_sum(offset, b):
-        return g[mine + b, :, halves[offset][1]].astype(F32) + gin[offset, b].astype(F32)
+        return g[b, :, halves[offset][1]].astype(F32) + gin[offset, b].astype(F32)
 
     def sum_blocks(offset, first, count, terms=()):
         def add(b, carry):
@@ -133,6 +132,7 @@
 
     ways = ((0, 2, 3, 1, 0, QUARTER), (1, 6, 5, 7, QUARTER, 0))
     arrivals = {}
+    load_g.wait()
     for way, own, three, step, both, alone in ways:
         halves[three][0].wait_recv()
         sum_blocks(three, alone, QUARTER)
@@ -169,6 +169,18 @@
     to_scalars.start()
     to_scalars.wait()
 
+    load_l.wait()
+    new_row = lax.broadcasted_iota(I32, (LANES, LANES), 0)
+    old_row = (new_row // 32) % 2 * NO + new_row % 32 * 2 + new_row // NO
+    reorder = jnp.where(lax.broadcasted_iota(I32, (LANES, LANES), 1) == old_row, 1.0, 0.0).astype(BF16)
+
+    def reorder_band(t, carry):
+        at = pl.ds(pl.multiple_of(t * LANES, LANES), LANES)
+        lv[at, :] = jnp.dot(reorder, lv[at, :], preferred_element_type=F32).astype(BF16)
+        return carry
+
+    lax.fori_loop(0, NY, reorder_band, 0)
+
     halves[0][0].wait_recv()
     for way in range(2):
         for part in ("near", "first", "last"):
@@ -202,7 +214,6 @@
 
     lax.fori_loop(0, NO - 1, dispatch, 0)
     pending.append(pltpu.make_async_copy(out1.at[pl.ds(0, NO - 1)], in1.at[pl.ds(0, NO - 1)], a1_s).wait)
-    load_l.wait()
     pltpu.make_async_copy(out1.at[pl.ds(0, NO - 1)], in1.at[pl.ds(0, NO - 1)], a1_r).wait()
 
     live_rows, live_cols = tab[2 + c, me], tab[4 + c, me]
@@ -224,14 +235,14 @@
         rows_of_band = lv[pl.ds(pl.multiple_of(t * LANES + half * NO, NO), NO), :]
         return jnp.dot(rows_of_band, masked, preferred_element_type=F32).astype(BF16)
 
-    def send_half(part, half):
-        at = pl.ds(pl.multiple_of(half * NO, NO), NO)
+    def send_half(half):
+        at = pl.ds(half * NO, NO)
         copies = []
         for i, offset in enumerate(FAR_FIRST):
             t = dp_at(offset)
-            prod[part, i] = half_band(t, half)
+            prod[half, i] = half_band(t, half)
             copy = remote(
-                prod.at[part, i], pin.at[at, my_tile], e_s.at[part, i], e_r.at[part, i], me, t * 2 + c
+                prod.at[half, i], pin.at[at, my_tile], e_s.at[half, i], e_r.at[half, i], me, t * 2 + c
             )
             copy.start()
             pending.append(copy.wait_send)
@@ -239,42 +250,49 @@
         pin[at, my_tile] = half_band(y, half)
         return copies
 
-    theirs_first = send_half(0, 1 - c)
-    mine_next = send_half(1, c)
+    sent = (send_half(0), send_half(1))
     load_r.wait()
-    for copy in theirs_first:
-        copy.wait_recv()
     column_limit = live_cols * LANES * jnp.where(y < live_rows, 1, 0)
     keep = lax.broadcasted_iota(I32, (NO, 8 * LANES), 1) < column_limit
 
-    def update(half):
-        rows_of_half = pin[pl.ds(pl.multiple_of(half * NO, NO), NO), :]
-        return jnp.where(keep, jnp.dot(rows_of_half, rv[...], preferred_element_type=F32), 0.0)
-
-    given = update(1 - c).astype(BF16)
-    for j in range(8):
-        dsc[j] = given[:, j * LANES : (j + 1) * LANES]
-    swap = remote(dsc, xin, x_s, x_r, me, other)
-    swap.start()
-    pending.append(swap.wait_send)
-    for copy in mine_next:
-        copy.wait_recv()
-    kept = update(c)
-    for j in range(8):
-        y32[pl.ds(c * 8 + j, NO, stride=16), :] = kept[:, j * LANES : (j + 1) * LANES]
-    swap.wait_recv()
-    for j in range(8):
-        y32[pl.ds((1 - c) * 8 + j, NO, stride=16), :] = xin[j].astype(F32)
-    out2[...] = y32[pl.ds(0, NO * 16), :].astype(BF16).reshape(NO, 16, LANES)
-
-    in2[me] = out2[me]
-
-    def give_back(i, carry):
-        t = owner_at(i)
-        remote(out2.at[t], in2.at[me], a2_s, a2_r, t, dp).start()
-        return carry
-
-    lax.fori_loop(0, NO - 1, give_back, 0)
+    for half in range(2):
+        for copy in sent[half]:
+            copy.wait_recv()
+        update = jnp.dot(pin[half * NO : (half + 1) * NO, :], rv[...], preferred_element_type=F32)
+        update = jnp.where(keep, update, 0.0).astype(BF16)
+        for to in range(2):
+            for j in range(8):
+                dsc[half, to, j] = update[to * 32 : (to + 1) * 32, j * LANES : (j + 1) * LANES]
+        swap = remote(dsc.at[half, 1 - c], xin.at[half], x_s.at[half], x_r.at[half], me, other)
+        swap.start()
+        pending.append(swap.wait_send)
+        for j in range(8):
+            y32[half, pl.ds(c * 8 + j, 32, stride=16), :] = dsc[half, c, j].astype(F32)
+        swap.wait_recv()
+        for j in range(8):
+            y32[half, pl.ds((1 - c) * 8 + j, 32, stride=16), :] = xin[half, j].astype(F32)
+        out2[half * 32 : (half + 1) * 32] = y32[half, pl.ds(0, 32 * 16), :].astype(BF16).reshape(32, 16, LANES)
+
+        odd = lax.rem(z + half, 2)
+
+        def give_back(i, carry, half=half, odd=odd):
+            u, v = lax.rem(i, 8), lax.div(i, 8)
+            there = lax.rem(x + far_first(u), 8)
+            depth = lax.rem(z + 4 + lax.div(v + 1, 2) * 2 * (1 - 2 * lax.rem(v, 2)) + 7 * odd, 8)
+            at = half * 32 + there * 4 + lax.div(depth, 2)
+            remote(out2.at[at], in2.at[me], a2_s, a2_r, there * 8 + depth, dp).start()
+            return carry
+
+        lax.fori_loop(0, 31, give_back, 0)
+
+        @pl.when(odd == 1)
+        def _(give_back=give_back):
+            give_back(31, 0)
+
+        @pl.when(odd == 0)
+        def _(half=half):
+            in2[me] = out2[half * 32 + lax.div(me, 2)]
+
     pending.append(pltpu.make_async_copy(out2.at[pl.ds(0, NO - 1)], in2.at[pl.ds(0, NO - 1)], a2_s).wait)
     pltpu.make_async_copy(out2.at[pl.ds(0, NO - 1)], in2.at[pl.ds(0, NO - 1)], a2_r).wait()
 
@@ -303,7 +321,7 @@
         in_specs=[any_spec, vmem_spec, vmem_spec, any_spec, any_spec],
         out_specs=vmem_spec,
         scratch_shapes=[
-            pltpu.VMEM((NB, 16, 8 * LANES), BF16),
+            pltpu.VMEM((HALF, 16, 8 * LANES), BF16),
             pltpu.VMEM((8, HALF, 16, LANES), BF16),
             pltpu.VMEM((8, HALF, 16, LANES), BF16),
             pltpu.VMEM((2, QUARTER, 16, LANES), BF16),
@@ -318,9 +336,9 @@
             pltpu.VMEM((8 * LANES + NO, LANES), F32),
             pltpu.VMEM((2, NY - 1, NO, LANES), BF16),
             pltpu.VMEM((LANES, 8 * LANES), BF16),
-            pltpu.VMEM((8, NO, LANES), BF16),
-            pltpu.VMEM((8, NO, LANES), BF16),
-            pltpu.VMEM((NO * 16 + 16, LANES), F32),
+            pltpu.VMEM((2, 2, 8, 32, LANES), BF16),
+            pltpu.VMEM((2, 8, 32, LANES), BF16),
+            pltpu.VMEM((2, 32 * 16 + 16, LANES), F32),
             pltpu.VMEM((NO, 16, LANES), BF16),
             pltpu.VMEM((NO, 16, LANES), BF16),
             pltpu.VMEM((NB * 8 + 8, LANES), F32),
@@ -334,7 +352,7 @@
             dma, dma,
             dma, dma,
             dma((2, 7)), dma((2, 7)),
-            dma, dma,
+            dma((2,)), dma((2,)),
             dma, dma,
         ],
         compiler_params=pltpu.CompilerParams(

time: 69.1 us -> 69 us (level)
  no operation moved by 1% of the time
where the time goes in v6:
time: 69 us; the launch traced here: 68.8 us
  Pallas kernels  67.2 us (97%)
  local copies, waits for them, and re-layouts  1.54 us (2%)
    pallas_call x1, Pallas kernels, on_device(): pl.pallas_call(kernel, out_shape=jax.ShapeDtypeStruct((NB, 8 * LANES), BF...  67.2 us
    unnamed x1, local copies, waits for them, and re-layouts  1.54 us

profile of v6, /device:TPU:1, one launch (start us, length us, event | category | flops | bytes accessed | tf_op | source)
XLA Modules:
  0.0 68.8 jit_solution(16569613643257875905)
XLA Ops:
  0.0 67.2 %shard_map.55 = bf16[48,1024]{1,0:T(8,128)(2,1)} custom-call(bf16[48,16,1024]{2,1,0:T(8,128)(2,1)} %bitcast.8, s32[1,48]{1,0:T(1,128)} %bitcast.11, s32[2,48]{1,0:T(2,128)} %bitcast.10, bf16[2,1024,1024]{2,1,0:T(8,128)(2,1)} %bitcast.6, bf16[2,1024,1024]{2,1,0:T(8,128)(2,1)} %bitcast.7), custom_call_target="tpu_custom_call" | custom-call | tf_op jit(solution)/shard_map/pallas_call | solution.py:318
  67.2 1.5 %copy.7 = bf16[48,1,1,1024]{3,0,2,1:T(8,128)(2,1)} copy(bf16[48,1,1,1024]{3,0,2,1:T(8,128)(2,1)} %bitcast.9) | data formatting | bytes 196608

commit v7 on v6

--- a/solution.py
+++ b/solution.py
@@ -69,7 +69,7 @@
     y, c = lax.div(dp, 2), lax.rem(dp, 2)
     other = dp + 1 - 2 * c
 
-    load_g = pltpu.make_async_copy(grads.at[pl.ds(c * HALF, HALF)], g, load_sem.at[0])
+    load_g = pltpu.make_async_copy(grads, g, load_sem.at[0])
     load_l = pltpu.make_async_copy(left.at[c], lv, load_sem.at[1])
     load_r = pltpu.make_async_copy(right.at[c], rv, load_sem.at[2])
     load_g.start()
@@ -96,11 +96,12 @@
     pl.semaphore_wait(barrier, 1 + 4 + 7)
 
     mine, theirs = c * HALF, (1 - c) * HALF
+    load_g.wait()
     halves = {}
     for offset in TILE_ORDER:
         tile = pl.ds(pl.multiple_of(dp_at(offset) * LANES, LANES), LANES)
         copy = remote(
-            grads.at[pl.ds(theirs, HALF), :, tile], gin.at[offset], core_s.at[offset], core_r.at[offset], me, other
+            g.at[pl.ds(theirs, HALF), :, tile], gin.at[offset], core_s.at[offset], core_r.at[offset], me, other
         )
         copy.start()
         pending.append(copy.wait_send)
@@ -110,7 +111,7 @@
     signal(plane.at[0], me, other)
 
     def core_sum(offset, b):
-        return g[b, :, halves[offset][1]].astype(F32) + gin[offset, b].astype(F32)
+        return g[mine + b, :, halves[offset][1]].astype(F32) + gin[offset, b].astype(F32)
 
     def sum_blocks(offset, first, count, terms=()):
         def add(b, carry):
@@ -132,7 +133,6 @@
 
     ways = ((0, 2, 3, 1, 0, QUARTER), (1, 6, 5, 7, QUARTER, 0))
     arrivals = {}
-    load_g.wait()
     for way, own, three, step, both, alone in ways:
         halves[three][0].wait_recv()
         sum_blocks(three, alone, QUARTER)
@@ -321,7 +321,7 @@
         in_specs=[any_spec, vmem_spec, vmem_spec, any_spec, any_spec],
         out_specs=vmem_spec,
         scratch_shapes=[
-            pltpu.VMEM((HALF, 16, 8 * LANES), BF16),
+            pltpu.VMEM((NB, 16, 8 * LANES), BF16),
             pltpu.VMEM((8, HALF, 16, LANES), BF16),
             pltpu.VMEM((8, HALF, 16, LANES), BF16),
             pltpu.VMEM((2, QUARTER, 16, LANES), BF16),

time: 69 us -> 69.3 us (level)
  no operation moved by 1% of the time
where the time goes in v7:
time: 69.3 us; the launch traced here: 69.1 us
  Pallas kernels  67.6 us (98%)
  local copies, waits for them, and re-layouts  1.54 us (2%)
    pallas_call x1, Pallas kernels, on_device(): pl.pallas_call(kernel, out_shape=jax.ShapeDtypeStruct((NB, 8 * LANES), BF...  67.6 us
    unnamed x1, local copies, waits for them, and re-layouts  1.54 us

profile of v7, /device:TPU:1, one launch (start us, length us, event | category | flops | bytes accessed | tf_op | source)
XLA Modules:
  0.0 69.1 jit_solution(8065725139554506543)
XLA Ops:
  0.0 67.6 %shard_map.55 = bf16[48,1024]{1,0:T(8,128)(2,1)} custom-call(bf16[48,16,1024]{2,1,0:T(8,128)(2,1)} %bitcast.8, s32[1,48]{1,0:T(1,128)} %bitcast.11, s32[2,48]{1,0:T(2,128)} %bitcast.10, bf16[2,1024,1024]{2,1,0:T(8,128)(2,1)} %bitcast.6, bf16[2,1024,1024]{2,1,0:T(8,128)(2,1)} %bitcast.7), custom_call_target="tpu_custom_call" | custom-call | tf_op jit(solution)/shard_map/pallas_call | solution.py:318
  67.6 1.5 %copy.7 = bf16[48,1,1,1024]{3,0,2,1:T(8,128)(2,1)} copy(bf16[48,1,1,1024]{3,0,2,1:T(8,128)(2,1)} %bitcast.9) | data formatting | bytes 196608
